TPU v7x, 32 devices: a whole 2x2x4 slice. The times are simulated.
32 devices in a mesh: tile: 4 (over y, core), rep: 8 (over z, x).
Axes of the slice: x: 2, y: 2, z: 4, core: 2. Of those that a mesh axis runs over, the one named last changes fastest.
Arguments:
- inputs: bfloat16 [8, 8, 32, 32, 256], P('rep', 'tile'), may hold values from -6 to 6
- grad_out: bfloat16 [8, 8, 32, 32, 256], P('rep', 'tile'), may hold values from -6 to 6
- seam_links: int32 [8, 4, 3], P('tile'), may hold values from 0 to 7, as said below
- corner_links: int32 [8, 4, 2], P('tile'), may hold values from 0 to 7, as said below
- dw_weight: float32 [256, 9], replicated, may hold values from -1 to 1
- norm_gain: float32 [256], replicated, may hold values from 0.1 to 1.9
- w_in: bfloat16 [256, 1024], replicated, may hold values from -0.375 to 0.375
- bias_in: float32 [1024], replicated, may hold values from -1 to 1
- w_out: bfloat16 [1024, 256], replicated, may hold values from -0.1875 to 0.1875
- layer_scale: float32 [256], replicated, may hold values from 0.25 to 2
Outputs:
- block_out: bfloat16 [8, 8, 32, 32, 256], P('rep', 'tile')
- x_grad: float32 [8, 8, 32, 32, 256], P('rep', 'tile')
- grad_dw: float32 [256, 9], replicated
- grad_gain: float32 [256], replicated
- grad_w_in: float32 [256, 1024], replicated
- grad_bias: float32 [1024], replicated
- grad_w_out: float32 [1024, 256], replicated
- grad_scale: float32 [256], replicated
Inputs may be any that keep to these rules, and one draw needn't show every extreme that they name: `seam_links`: entry [t, s] = (t2, s2, f): side s of tile t meets side s2 of tile t2, reversed if f = 1. Sides are paired: entry [t2, s2] = (t, s, f), and no entry names its own side. `corner_links`: entry [t, k] = (t2, k2): corner k of tile t meets corner k2 of tile t2. Corners are paired: entry [t2, k2] = (t, k), and no entry names its own corner.
All inputs are finite; a program needn't handle non-finite values.
Results may differ from a plain program's by a relative error of at most 0.0063.
Values may be sent and summed in bfloat16 or wider, within the bound.
A program may use at most 64 MiB of HBM per device.

v0:
```python
import math
import jax
import jax.numpy as jnp
from jax import lax
from jax.sharding import PartitionSpec as P

INV_ROOT_TWO = 0.7071067811865476
INV_ROOT_TAU = 0.3989422804014327


def edge_strips(blocks):
    top_row = blocks[..., 0, :, :]
    right_col = blocks[..., :, -1, :]
    bottom_row = blocks[..., -1, ::-1, :]
    left_col = blocks[..., ::-1, 0, :]
    return jnp.stack([top_row, right_col, bottom_row, left_col], axis=-3)


def corner_cells(blocks):
    return jnp.stack(
        [
            blocks[..., 0, 0, :],
            blocks[..., 0, -1, :],
            blocks[..., -1, -1, :],
            blocks[..., -1, 0, :],
        ],
        axis=-2,
    )


def fetch_linked(all_strips, all_points, seam_links, corner_links):
    picked = all_strips[:, seam_links[..., 0], seam_links[..., 1]]
    reverse = (seam_links[..., 2] == 1)[None, :, :, None, None]
    strips = jnp.where(reverse, picked[..., ::-1, :], picked)
    points = all_points[:, corner_links[..., 0], corner_links[..., 1]]
    return (strips, points)


def assemble(blocks, strips, points):
    top_row = jnp.concatenate(
        [points[..., 0:1, :], strips[..., 0, :, :], points[..., 1:2, :]], axis=-2
    )
    bottom_row = jnp.concatenate(
        [points[..., 3:4, :], strips[..., 2, ::-1, :], points[..., 2:3, :]], axis=-2
    )
    left_col = strips[..., 3, ::-1, :][..., :, None, :]
    right_col = strips[..., 1, :, :][..., :, None, :]
    middle = jnp.concatenate([left_col, blocks, right_col], axis=-2)
    return jnp.concatenate([top_row[..., None, :, :], middle, bottom_row[..., None, :, :]], axis=-3)


def padded_parts(grad_padded):
    interior = grad_padded[..., 1:-1, 1:-1, :]
    top_row = grad_padded[..., 0, 1:-1, :]
    right_col = grad_padded[..., 1:-1, -1, :]
    bottom_row = grad_padded[..., -1, 1:-1, :][..., ::-1, :]
    left_col = grad_padded[..., 1:-1, 0, :][..., ::-1, :]
    strips = jnp.stack([top_row, right_col, bottom_row, left_col], axis=-3)
    points = jnp.stack(
        [
            grad_padded[..., 0, 0, :],
            grad_padded[..., 0, -1, :],
            grad_padded[..., -1, -1, :],
            grad_padded[..., -1, 0, :],
        ],
        axis=-2,
    )
    return (interior, strips, points)


def add_to_rims(target, strips, points):
    extent = target.shape[-2]
    row_ids = lax.broadcasted_iota(jnp.int32, (extent, 1, 1), 0)
    col_ids = lax.broadcasted_iota(jnp.int32, (1, extent, 1), 1)
    top_mask = row_ids == 0
    bottom_mask = row_ids == extent - 1
    left_mask = col_ids == 0
    right_mask = col_ids == extent - 1
    target = target + jnp.where(top_mask, strips[..., 0, :, :][..., None, :, :], 0.0)
    target = target + jnp.where(right_mask, strips[..., 1, :, :][..., :, None, :], 0.0)
    target = target + jnp.where(bottom_mask, strips[..., 2, ::-1, :][..., None, :, :], 0.0)
    target = target + jnp.where(left_mask, strips[..., 3, ::-1, :][..., :, None, :], 0.0)
    target = target + jnp.where(top_mask & left_mask, points[..., 0, :][..., None, None, :], 0.0)
    target = target + jnp.where(top_mask & right_mask, points[..., 1, :][..., None, None, :], 0.0)
    target = target + jnp.where(
        bottom_mask & right_mask, points[..., 2, :][..., None, None, :], 0.0
    )
    target = target + jnp.where(bottom_mask & left_mask, points[..., 3, :][..., None, None, :], 0.0)
    return target


def forward_backward(
    padded, blocks, grad_out, dw_weight, norm_gain, w_in, bias_in, w_out, layer_scale
):
    extent = blocks.shape[-2]
    channels = blocks.shape[-1]
    mixed_cells = jnp.zeros(blocks.shape, jnp.float32)
    for row_off in range(3):
        for col_off in range(3):
            tap_index = 3 * row_off + col_off
            window = padded[..., row_off : row_off + extent, col_off : col_off + extent, :].astype(
                jnp.float32
            )
            mixed_cells = mixed_cells + window * dw_weight[:, tap_index]
    average = jnp.mean(mixed_cells, axis=-1, keepdims=True)
    centred = mixed_cells - average
    inv_std = lax.rsqrt(jnp.mean(centred * centred, axis=-1, keepdims=True) + 1e-06)
    standard = centred * inv_std
    normed = (standard * norm_gain).astype(jnp.bfloat16).reshape(-1, channels)
    hidden_pre = jnp.dot(normed, w_in, preferred_element_type=jnp.float32) + bias_in
    activated = jax.nn.gelu(hidden_pre, approximate=False).astype(jnp.bfloat16)
    branch = jnp.dot(activated, w_out, preferred_element_type=jnp.float32)
    cotangent = grad_out.reshape(-1, channels).astype(jnp.float32)
    block_out = (
        (blocks.reshape(-1, channels).astype(jnp.float32) + layer_scale * branch)
        .astype(jnp.bfloat16)
        .reshape(blocks.shape)
    )
    grad_scale = jnp.sum(cotangent * branch, axis=0)
    grad_mix = (cotangent * layer_scale).astype(jnp.bfloat16)
    grad_w_out = lax.dot_general(
        activated, grad_mix, (((0,), (0,)), ((), ())), preferred_element_type=jnp.float32
    )
    grad_act = lax.dot_general(
        grad_mix, w_out, (((1,), (1,)), ((), ())), preferred_element_type=jnp.float32
    )
    gelu_slope = (
        0.5 * (1.0 + lax.erf(hidden_pre * INV_ROOT_TWO))
        + hidden_pre * jnp.exp(-0.5 * hidden_pre * hidden_pre) * INV_ROOT_TAU
    )
    grad_hidden = (grad_act * gelu_slope).astype(jnp.bfloat16)
    grad_bias = jnp.sum(grad_hidden.astype(jnp.float32), axis=0)
    grad_w_in = lax.dot_general(
        normed, grad_hidden, (((0,), (0,)), ((), ())), preferred_element_type=jnp.float32
    )
    grad_normed = lax.dot_general(
        grad_hidden, w_in, (((1,), (1,)), ((), ())), preferred_element_type=jnp.float32
    ).reshape(blocks.shape)
    grad_gain = jnp.sum((grad_normed * standard).reshape(-1, channels), axis=0)
    grad_unit = grad_normed * norm_gain
    grad_mixed = (
        grad_unit
        - jnp.mean(grad_unit, axis=-1, keepdims=True)
        - standard * jnp.mean(grad_unit * standard, axis=-1, keepdims=True)
    ) * inv_std
    pad_widths = [(0, 0)] * (grad_mixed.ndim - 3) + [(2, 2), (2, 2), (0, 0)]
    wide_grad = jnp.pad(grad_mixed, pad_widths)
    grad_padded = jnp.zeros(padded.shape, jnp.float32)
    dw_columns = []
    for row_off in range(3):
        for col_off in range(3):
            tap_index = 3 * row_off + col_off
            window = padded[..., row_off : row_off + extent, col_off : col_off + extent, :].astype(
                jnp.float32
            )
            shifted = wide_grad[
                ..., 2 - row_off : 4 - row_off + extent, 2 - col_off : 4 - col_off + extent, :
            ]
            grad_padded = grad_padded + shifted * dw_weight[:, tap_index]
            dw_columns.append(jnp.sum((grad_mixed * window).reshape(-1, channels), axis=0))
    grad_dw = jnp.stack(dw_columns, axis=1)
    return (
        block_out,
        grad_padded,
        (grad_dw, grad_gain, grad_w_in, grad_bias, grad_w_out, grad_scale),
    )


def body(
    inputs,
    grad_out,
    seam_links,
    corner_links,
    dw_weight,
    norm_gain,
    w_in,
    bias_in,
    w_out,
    layer_scale,
):
    all_strips, all_points = (
        lax.all_gather(edge_strips(inputs), "tile", axis=1, tiled=True),
        lax.all_gather(corner_cells(inputs), "tile", axis=1, tiled=True),
    )
    strips, points = fetch_linked(all_strips, all_points, seam_links, corner_links)
    padded = assemble(inputs, strips, points)
    block_out, grad_padded, partials = forward_backward(
        padded, inputs, grad_out, dw_weight, norm_gain, w_in, bias_in, w_out, layer_scale
    )
    grad_dw, grad_gain, grad_w_in, grad_bias, grad_w_out, grad_scale = partials
    interior, back_strips, back_points = padded_parts(grad_padded)
    home_strips, home_points = (
        lax.all_gather(back_strips.astype(jnp.bfloat16), "tile", axis=1, tiled=True).astype(
            back_strips.dtype
        ),
        lax.all_gather(back_points.astype(jnp.bfloat16), "tile", axis=1, tiled=True).astype(
            back_points.dtype
        ),
    )
    return_strips, return_points = fetch_linked(home_strips, home_points, seam_links, corner_links)
    x_grad = add_to_rims(grad_out.astype(jnp.float32) + interior, return_strips, return_points)
    cell_total = (
        lax.axis_size("tile")
        * lax.axis_size("rep")
        * inputs.shape[0]
        * inputs.shape[1]
        * inputs.shape[2]
        * inputs.shape[3]
    )
    factor = 1.0 / math.sqrt(cell_total)
    summed = lax.psum(
        (grad_dw, grad_gain, grad_w_in, grad_bias, grad_w_out, grad_scale), ("tile", "rep")
    )
    return (
        block_out,
        x_grad,
        summed[0] * factor,
        summed[1] * factor,
        summed[2] * factor,
        summed[3] * factor,
        summed[4] * factor,
        summed[5] * factor,
    )


def solution(mesh):
    placed = (
        P("rep", "tile", None, None, None),
        P("rep", "tile", None, None, None),
        P("tile", None, None),
        P("tile", None, None),
        P(),
        P(),
        P(),
        P(),
        P(),
        P(),
    )
    return jax.shard_map(
        body,
        mesh=mesh,
        in_specs=placed,
        out_specs=(
            P("rep", "tile", None, None, None),
            P("rep", "tile", None, None, None),
            P(),
            P(),
            P(),
            P(),
            P(),
            P(),
        ),
        check_vma=False,
    )
```

profile of v0, /device:TPU:0, one launch (start us, length us, event | category | flops | bytes accessed | tf_op | source)
XLA Modules:
  0.0 216.6 jit_solution(4268885214619424398)
XLA Ops:
  7.3 0.9 fusion.76
  8.1 1.1 fusion.75
  9.3 0.8 slice_bitcast_fusion.8
  11.5 6.2 %all_gather.12 = bf16[1,8,4,256]{3,2,0,1:T(4,128)(2,1)S(1)} all-gather(bf16[1,2,4,256]{3,2,0,1:T(4,128)(2,1)S(1)} %copy.212), channel_id=1, replica_groups=mesh['tile'=4,'rep'=8] {'tile'}, dimensions={1}, use_global_device_ids=true | all-gather | bytes 20480 | tf_op jit(solution)/shard_map/all_gather | solution.py:183
  17.7 0.8 fusion.71
  19.4 7.6 %all_gather.13 = bf16[1,8,4,32,256]{4,3,1,2,0:T(8,128)(2,1)S(1)} all-gather(bf16[1,2,4,32,256]{4,3,1,2,0:T(8,128)(2,1)S(1)} %pad_maximum_fusion.3), channel_id=1, replica_groups=mesh['tile'=4,'rep'=8] {'tile'}, dimensions={1}, use_global_device_ids=true | all-gather | bytes 655360 | tf_op jit(solution)/shard_map/all_gather | solution.py:182
  28.4 1.7 maximum_maximum_fusion
  30.1 5.2 %fusion.72 = (f32[2,32,32]{2,1,0:T(8,128)S(1)}, f32[1,2,32,32,256]{4,3,2,1,0:T(8,128)S(1)}) fusion(f32[256]{0:T(256)S(1)} %bitcast.170, bf16[1,2,33,34,256]{4,3,2,1,0:T(8,128)(2,1)S(1)} %get-tuple-element.81, f32[256]{0:T(256)S(1)} %bitcast.172, f32[256]{0:T(256)S(1)} %bitcast.158, f32[256]{0:T(256)S(1)} %bitcast.160, ...), kind=kLoop, calls=%fused_computation.185 | loop fusion | flops 17299456 | bytes 9520128 | tf_op jit(solution)/shard_map/reduce_sum | solution.py:105
  36.0 0.7 multiply_convert_fusion
  36.8 19.3 %fusion.2 = (bf16[2048,1024]{1,0:T(8,128)(2,1)S(1)}, f32[2048,1024]{1,0:T(8,128)S(1)}) fusion(f32[1024]{0:T(1024)S(1)} %copy-done.13, bf16[2048,256]{1,0:T(8,128)(2,1)S(1)} %bitcast.144, bf16[256,1024]{1,0:T(8,128)(2,1)S(1)} %copy-done), kind=kOutput, calls=%fused_computation.8 | convolution fusion | flops 1212153856 | bytes 14159872 | tf_op jit(solution)/shard_map/dot_general | solution.py:110
  56.2 3.1 %fusion.58 = (f32[256]{0:T(256)}, bf16[2048,256]{1,0:T(8,128)(2,1)}, bf16[2048,256]{1,0:T(8,128)(2,1)S(1)}) fusion(bf16[1,2,32,32,256]{4,3,2,1,0:T(8,128)(2,1)S(1)} %copy-done.6, f32[256]{0:T(256)S(1)} %copy-done.14, bf16[1,2,32,32,256]{4,3,2,1,0:T(8,128)(2,1)S(1)} %copy-done.5, bf16[2048,1024]{1,0:T(8,128)(2,1)S(1)} %get-tuple-element.122, ...), kind=kOutput, calls=%fused_computation.102 | convolution fusion | flops 1078460160 | bytes 8914944 | tf_op jit(solution)/shard_map/dot_general | solution.py:112
  59.3 2.2 %fusion.82 = f32[1024,256]{1,0:T(8,128)} fusion(bf16[2048,1024]{1,0:T(8,128)(2,1)S(1)} %get-tuple-element.122, bf16[2048,256]{1,0:T(8,128)(2,1)S(1)} %get-tuple-element.82), kind=kOutput, calls=%fused_computation.194 | convolution fusion | flops 1073741824 | bytes 6291456 | tf_op jit(solution)/shard_map/dot_general | solution.py:121
  61.5 4.9 %convert_reduce_fusion = (f32[1024]{0:T(1024)S(1)}, bf16[2048,1024]{1,0:T(8,128)(2,1)S(1)}) fusion(f32[2048,1024]{1,0:T(8,128)S(1)} %get-tuple-element.123, f32[1024]{0:T(1024)S(1)} %copy-done.13, bf16[2048,256]{1,0:T(8,128)(2,1)S(1)} %get-tuple-element.82, bf16[1024,256]{1,0:T(8,128)(2,1)S(1)} %copy-done.12), kind=kOutput, calls=%fused_computation.15 | convolution fusion | flops 1101003776 | bytes 14163968 | tf_op jit(solution)/shard_map/dot_general | solution.py:124
  66.4 1.9 copy-done.15
  68.3 2.2 %fusion.81 = f32[256,1024]{1,0:T(8,128)} fusion(bf16[2048,256]{1,0:T(8,128)(2,1)S(1)} %bitcast.145, bf16[2048,1024]{1,0:T(8,128)(2,1)S(1)} %get-tuple-element.127), kind=kOutput, calls=%fused_computation.193 | convolution fusion | flops 1073741824 | bytes 6291456 | tf_op jit(solution)/shard_map/dot_general | solution.py:133
  70.6 3.6 %multiply_reduce_fusion.3 = (f32[2048]{0:T(1024)S(1)}, f32[2048,256]{1,0:T(8,128)S(1)}) fusion(f32[256]{0:T(256)S(1)} %copy-done.9, bf16[2048,1024]{1,0:T(8,128)(2,1)} %copy-done.15, bf16[256,1024]{1,0:T(8,128)(2,1)S(1)} %copy-done), kind=kOutput, calls=%fused_computation.109 | convolution fusion | flops 1074788352 | bytes 6824960 | tf_op jit(solution)/shard_map/dot_general | solution.py:136
  74.2 1.1 multiply_reduce_fusion
  75.6 8.3 %fusion.48 = (f32[256]{0:T(256)S(1)}, f32[256]{0:T(256)S(1)}, f32[256]{0:T(256)S(1)}, f32[256]{0:T(256)S(1)}, f32[256]{0:T(256)S(1)}, /*index=5*/f32[256]{0:T(25...) fusion(bf16[1,2,33,34,256]{4,3,2,1,0:T(8,128)(2,1)} %copy-done.2, ...), kind=kLoop, calls=%fused_computation.89 | loop fusion | flops 20969216 | bytes 13740032 | tf_op jit(solution)/shard_map/reduce_sum | solution.py:160
  83.9 2.8 %fusion.24 = f32[1,2,34,34,256]{4,3,2,1,0:T(8,128)S(1)} fusion(f32[1,2,32,32,256]{4,3,2,1,0:T(8,128)S(1)} %get-tuple-element.71, f32[256]{0:T(256)S(1)} %bitcast.171, f32[256]{0:T(256)S(1)} %bitcast.173, f32[256]{0:T(256)S(1)} %bitcast.159, f32[256]{0:T(256)S(1)} %bitcast.161, f32[256]{0:T(256)S(1)} %bitcast.163, f32[256]{0:T(256)S(1)} %bitcast.165, ...), kind=kLoop, calls=%fused_computation.48 | loop fusion | flops 10061824 | bytes 4473856 | tf_op jit(solution)/shard_map/add | solution.py:159
  88.7 40.9 %all-reduce.1 = (f32[256,9]{0,1:T(8,128)}, f32[256]{0:T(256)S(1)}, f32[1024]{0:T(1024)S(1)}, f32[256]{0:T(256)S(1)}) all-reduce(f32[256,9]{0,1:T(8,128)S(1)} %stack.78, f32[256]{0:T(256)S(1)} %get-tuple-element.57, f32[1024]{0:T(1024)S(1)} %get-tuple-element.126, ...), channel_id=1, replica_groups=mesh['tile'=4,'rep'=8] {'tile','rep'}, use_global_device_ids=true, to_apply=%region_13.14 | all-reduce | flops 3840 | bytes 30720 | tf_op jit(solution)/shard_map/psum | solution.py:211
  131.6 0.8 pad_maximum_fusion.4
  132.4 8.5 %all_gather.14 = bf16[1,8,4,32,256]{4,3,2,0,1:T(8,128)(2,1)S(1)} all-gather(bf16[1,2,4,32,256]{4,3,2,0,1:T(8,128)(2,1)S(1)} %copy.228), channel_id=1, replica_groups=mesh['tile'=4,'rep'=8] {'tile'}, dimensions={1}, use_global_device_ids=true | all-gather | bytes 655360 | tf_op jit(solution)/shard_map/all_gather | solution.py:193
  140.9 1.1 bitcast_convert_fusion
  142.0 2.5 %gather_fusion.2 = f32[8,32,256]{2,1,0:T(8,128)} fusion(f32[8,4,32,256]{3,2,1,0:T(8,128)} %bitcast_convert_fusion, s32[8]{0:T(128)S(1)} %reshape.484), kind=kCustom, calls=%fused_computation.2 | custom fusion | bytes 524352 | tf_op jit(solution)/shard_map/gather | solution.py:32
  144.5 1.6 rev.37
  146.1 1.1 broadcast_select_fusion
  148.6 5.2 %all_gather.15 = bf16[1,8,4,256]{3,2,0,1:T(4,128)(2,1)S(1)} all-gather(bf16[1,2,4,256]{3,2,0,1:T(4,128)(2,1)S(1)} %copy.230), channel_id=1, replica_groups=mesh['tile'=4,'rep'=8] {'tile'}, dimensions={1}, use_global_device_ids=true | all-gather | bytes 20480 | tf_op jit(solution)/shard_map/all_gather | solution.py:196
  154.5 0.8 rev.39
  156.0 4.5 %fusion.56 = f32[1,2,32,32,256]{4,3,2,1,0:T(8,128)} fusion(f32[1,2,34,34,256]{4,3,2,1,0:T(8,128)S(1)} %fusion.24, bf16[1,2,32,32,256]{4,3,2,1,0:T(8,128)(2,1)} %param.11, f32[2,256]{1,0:T(2,128)S(1)} %bitcast.174, f32[2,256]{1,0:T(2,128)S(1)} %bitcast.175, f32[2,256]{1,0:T(2,128)S(1)} %bitcast.176, f32[2,256]{1,0:T(2,128)S(1)} %bitcast.177, ...), kind=kLoop, calls=%fused_computation.98 | loop fusion | flops 9437184 | bytes 5531648 | tf_op jit(solution)/shard_map/add | solution.py:88
  160.5 45.8 %all-reduce.5.cloned.1.call-done = (f32[256,1024]{1,0:T(8,128)}, f32[1024,256]{1,0:T(8,128)}) async-done(((f32[256,1024]{1,0:T(8,128)}, f32[1024,256]{1,0:T(8,128)}), (f32[256,1024]{1,0:T(8,128)}, f32[1024,256]{1,0:T(8,128)})) %all-reduce.5.cloned.1.call-update) | async-done | bytes 2097168 | tf_op jit(solution)/shard_map/psum | solution.py:211
  206.3 2.4 %broadcast_multiply_fusion = f32[1024,256]{1,0:T(8,128)} fusion(f32[1024,256]{1,0:T(8,128)} %get-tuple-element.70), kind=kLoop, calls=%fused_computation.118 | loop fusion | flops 262144 | bytes 2097152 | tf_op jit(solution)/shard_map/mul | solution.py:221
  208.6 1.1 broadcast_multiply_fusion.1
  (101 shorter events, 11.2 us)
Async XLA Ops:
  7.2 29.6 %copy-start = (bf16[256,1024]{1,0:T(8,128)(2,1)S(1)}, bf16[256,1024]{1,0:T(8,128)(2,1)}, u32[]{:S(2)}) copy-start(bf16[256,1024]{1,0:T(8,128)(2,1)} %param.16) | copy-start | bytes 1572868
  7.2 21.2 %copy-start.4 = (bf16[1,2,32,32,256]{4,3,2,1,0:T(8,128)(2,1)S(1)}, bf16[1,2,32,32,256]{4,3,2,1,0:T(8,128)(2,1)}, u32[]{:S(2)}) copy-start(bf16[1,2,32,32,256]{4,3,2,1,0:T(8,128)(2,1)} %param.10) | copy-start | bytes 3145732
  7.2 21.1 %copy-start.10 = (f32[256,9]{0,1:T(8,128)S(1)}, f32[256,9]{0,1:T(8,128)}, u32[]{:S(2)}) copy-start(f32[256,9]{0,1:T(8,128)} %param.14) | copy-start | bytes 27652
  7.2 199.1 %all-reduce.5.cloned.1.call-start = ((), (), s32[]{:S(2)}) async-start(), calls=%async_computation | async-start | bytes 4194304 | tf_op jit(solution)/shard_map/psum | solution.py:211
  11.4 16.4 %copy-start.11 = (pred[2,4]{1,0:T(4,128)(4,1)}, pred[2,4]{1,0:T(4,128)(4,1)S(1)}, u32[]{:S(2)}) copy-start(pred[2,4]{1,0:T(4,128)(4,1)S(1)} %compare_bitcast_fusion) | copy-start | bytes 28
  30.1 5.2 %copy-start.1 = (bf16[1,2,33,34,256]{4,3,2,1,0:T(8,128)(2,1)}, bf16[1,2,33,34,256]{4,3,2,1,0:T(8,128)(2,1)S(1)}, u32[]{:S(2)}) copy-start(bf16[1,2,33,34,256]{4,3,2,1,0:T(8,128)(2,1)S(1)} %get-tuple-element.80) | copy-start | bytes 3446788
  30.1 5.2 %copy-start.2 = (bf16[1,2,33,34,256]{4,3,2,1,0:T(8,128)(2,1)}, bf16[1,2,33,34,256]{4,3,2,1,0:T(8,128)(2,1)S(1)}, u32[]{:S(2)}) copy-start(bf16[1,2,33,34,256]{4,3,2,1,0:T(8,128)(2,1)S(1)} %get-tuple-element.81) | copy-start | bytes 3446788
  30.1 5.9 %copy-start.9 = (f32[256]{0:T(256)S(1)}, f32[256]{0:T(256)}, u32[]{:S(2)}) copy-start(f32[256]{0:T(256)} %param.15) | copy-start | bytes 3076
  35.3 1.4 copy-start.13
  36.8 19.4 %copy-start.5 = (bf16[1,2,32,32,256]{4,3,2,1,0:T(8,128)(2,1)S(1)}, bf16[1,2,32,32,256]{4,3,2,1,0:T(8,128)(2,1)}, u32[]{:S(2)}) copy-start(bf16[1,2,32,32,256]{4,3,2,1,0:T(8,128)(2,1)} %param.10) | copy-start | bytes 3145732
  36.8 19.4 %copy-start.6 = (bf16[1,2,32,32,256]{4,3,2,1,0:T(8,128)(2,1)S(1)}, bf16[1,2,32,32,256]{4,3,2,1,0:T(8,128)(2,1)}, u32[]{:S(2)}) copy-start(bf16[1,2,32,32,256]{4,3,2,1,0:T(8,128)(2,1)} %param.11) | copy-start | bytes 3145732
  36.8 19.4 %copy-start.12 = (bf16[1024,256]{1,0:T(8,128)(2,1)S(1)}, bf16[1024,256]{1,0:T(8,128)(2,1)}, u32[]{:S(2)}) copy-start(bf16[1024,256]{1,0:T(8,128)(2,1)} %param.18) | copy-start | bytes 1572868
  36.8 19.4 %copy-start.14 = (f32[256]{0:T(256)S(1)}, f32[256]{0:T(256)}, u32[]{:S(2)}) copy-start(f32[256]{0:T(256)} %param.19) | copy-start | bytes 3076
  66.4 1.9 copy-start.15
  74.2 1.3 copy-start.3
  132.3 23.1 %copy-start.8 = (f32[256,9]{0,1:T(8,128)S(1)}, f32[256,9]{0,1:T(8,128)}, u32[]{:S(2)}) copy-start(f32[256,9]{0,1:T(8,128)} %get-tuple-element.65) | copy-start | bytes 27652
  206.3 2.4 %copy-start.7 = (f32[256,1024]{1,0:T(8,128)S(1)}, f32[256,1024]{1,0:T(8,128)}, u32[]{:S(2)}) copy-start(f32[256,1024]{1,0:T(8,128)} %get-tuple-element.69) | copy-start | bytes 3145732
Sparse Core Ops, SparseCore 0:
  70.7 135.4 all-reduce.4
where the time goes:
time: 217 us
  blocking collectives  68.5 us (32%)
  waiting for transfers between devices  45.8 us (21%)
  other arithmetic  35.4 us (16%)
  matrix products  35.4 us (16%)
  local copies, waits for them, and re-layouts  16.8 us (8%)
  between operations  14.6 us (7%)
    psum x1, waiting for transfers between devices, body(): lax.psum((grad_dw, grad_gain, grad_w_in, grad_bias, grad_w_out, grad_scal...  45.8 us
    psum x1, blocking collectives, body(): lax.psum((grad_dw, grad_gain, grad_w_in, grad_bias, grad_w_out, grad_scal...  40.9 us
    dot_general x1, matrix products, forward_backward(): jnp.dot(normed, w_in, preferred_element_type=jnp.float32) + bias_in  19.3 us
    all_gather x1, blocking collectives, body(): lax.all_gather(back_strips.astype(jnp.bfloat16), 'tile', axis=1, tiled=True)  8.53 us
    reduce_sum x1, other arithmetic, forward_backward(): jnp.sum((grad_mixed * window).reshape(-1, channels), axis=0)  8.32 us
    all_gather x1, blocking collectives, body(): lax.all_gather(edge_strips(inputs), 'tile', axis=1, tiled=True)  7.62 us
    all_gather x1, blocking collectives, body(): lax.all_gather(corner_cells(inputs), 'tile', axis=1, tiled=True)  6.22 us
    all_gather x1, blocking collectives, body(): lax.all_gather(back_points.astype(jnp.bfloat16), 'tile', axis=1, tiled=True)  5.19 us
  transfers between devices with their start and end apart: 1, of which 1 were waited for; matrix products, arithmetic and copies ran while one was open for 16% of the time, Pallas kernels for 0%

commit v1 on v0

--- a/solution.py
+++ b/solution.py
@@ -6,6 +6,28 @@
 
 INV_ROOT_TWO = 0.7071067811865476
 INV_ROOT_TAU = 0.3989422804014327
+
+
+def joined_along(blocks, dim):
+    blocks = jnp.moveaxis(blocks, 0, dim)
+    dims = blocks.shape
+    return blocks.reshape(*dims[:dim], dims[dim] * dims[dim + 1], *dims[dim + 2 :])
+
+
+def collected_by_bits(value, axis):
+    peers = lax.axis_size(axis)
+    blocks = value[None]
+    for level in range(peers.bit_length() - 1):
+        bit = 1 << level
+        received = lax.ppermute(blocks, axis, [(i, i ^ bit) for i in range(peers)])
+        both = jnp.stack([blocks, received])
+        upper = lax.axis_index(axis) >> level & 1
+        blocks = jnp.where(upper == 0, both, both[::-1]).reshape(-1, *value.shape)
+    return blocks
+
+
+def collect(shard, axis, dim):
+    return joined_along(collected_by_bits(shard, axis), dim)
 
 
 def edge_strips(blocks):
@@ -193,9 +215,7 @@
         lax.all_gather(back_strips.astype(jnp.bfloat16), "tile", axis=1, tiled=True).astype(
             back_strips.dtype
         ),
-        lax.all_gather(back_points.astype(jnp.bfloat16), "tile", axis=1, tiled=True).astype(
-            back_points.dtype
-        ),
+        collect(back_points.astype(jnp.bfloat16), "tile", 1).astype(back_points.dtype),
     )
     return_strips, return_points = fetch_linked(home_strips, home_points, seam_links, corner_links)
     x_grad = add_to_rims(grad_out.astype(jnp.float32) + interior, return_strips, return_points)

time: 217 us -> 232 us (1.069)
  waiting for transfers between devices: 45.8 us -> 65.9 us
  blocking collectives: 68.5 us -> 62.9 us
  other arithmetic: 35.4 us -> 38.2 us
    psum x1, waiting for transfers between devices: 45.8 us -> 64.4 us  [body(): lax.psum((grad_dw, grad_gain, grad_w_in, grad_bias, grad_w_out, grad_scal...]
    all_gather x1 -> x0, blocking collectives: 5.19 us -> none  [body(): lax.all_gather(back_points.astype(jnp.bfloat16), 'tile', axis=1, tiled=True)]
  transfers between devices with their start and end apart: 1 -> 3, of which waited for: 1 -> 2; matrix products, arithmetic and copies ran while one was open for 16% -> 11% of each run, Pallas kernels for 0% -> 0%
where the time goes in v1:
time: 232 us
  waiting for transfers between devices  65.9 us (28%)
  blocking collectives  62.9 us (27%)
  other arithmetic  38.2 us (16%)
  matrix products  33.8 us (15%)
  local copies, waits for them, and re-layouts  14.8 us (6%)
  between operations  14.7 us (6%)
    psum x1, waiting for transfers between devices, body(): lax.psum((grad_dw, grad_gain, grad_w_in, grad_bias, grad_w_out, grad_scal...  64.4 us
    psum x1, blocking collectives, body(): lax.psum((grad_dw, grad_gain, grad_w_in, grad_bias, grad_w_out, grad_scal...  41.3 us
    dot_general x1, matrix products, forward_backward(): jnp.dot(normed, w_in, preferred_element_type=jnp.float32) + bias_in  19.3 us
    reduce_sum x1, other arithmetic, forward_backward(): jnp.sum((grad_mixed * window).reshape(-1, channels), axis=0)  8.46 us
    all_gather x1, blocking collectives, body(): lax.all_gather(back_strips.astype(jnp.bfloat16), 'tile', axis=1, tiled=True)  7.73 us
    all_gather x1, blocking collectives, body(): lax.all_gather(edge_strips(inputs), 'tile', axis=1, tiled=True)  7.62 us
    all_gather x1, blocking collectives, body(): lax.all_gather(corner_cells(inputs), 'tile', axis=1, tiled=True)  6.22 us
    dot_general x1, matrix products, forward_backward(): lax.dot_general(grad_mix, w_out, (((1,), (1,)), ((), ())), preferred_elem...  5.46 us
  transfers between devices with their start and end apart: 3, of which 2 were waited for; matrix products, arithmetic and copies ran while one was open for 11% of the time, Pallas kernels for 0%

profile of v1, /device:TPU:0, one launch (start us, length us, event | category | flops | bytes accessed | tf_op | source)
XLA Modules:
  0.0 231.6 jit_solution(8172390650465405180)
XLA Ops:
  7.2 0.9 fusion.85
  8.1 1.1 fusion.84
  9.3 0.8 slice_bitcast_fusion.8
  11.5 6.2 %all_gather.9 = bf16[1,8,4,256]{3,2,0,1:T(4,128)(2,1)S(1)} all-gather(bf16[1,2,4,256]{3,2,0,1:T(4,128)(2,1)S(1)} %copy.252), channel_id=1, replica_groups=mesh['tile'=4,'rep'=8] {'tile'}, dimensions={1}, use_global_device_ids=true | all-gather | bytes 20480 | tf_op jit(solution)/shard_map/all_gather | solution.py:205
  17.7 0.8 fusion.81
  19.4 7.6 %all_gather.10 = bf16[1,8,4,32,256]{4,3,1,2,0:T(8,128)(2,1)S(1)} all-gather(bf16[1,2,4,32,256]{4,3,1,2,0:T(8,128)(2,1)S(1)} %pad_maximum_fusion.3), channel_id=1, replica_groups=mesh['tile'=4,'rep'=8] {'tile'}, dimensions={1}, use_global_device_ids=true | all-gather | bytes 655360 | tf_op jit(solution)/shard_map/all_gather | solution.py:204
  28.4 1.7 maximum_maximum_fusion
  30.1 5.2 %fusion.82 = (f32[2,32,32]{2,1,0:T(8,128)S(1)}, f32[1,2,32,32,256]{4,3,2,1,0:T(8,128)S(1)}) fusion(f32[256]{0:T(256)S(1)} %bitcast.180, bf16[1,2,33,34,256]{4,3,2,1,0:T(8,128)(2,1)S(1)} %get-tuple-element.85, f32[256]{0:T(256)S(1)} %bitcast.182, f32[256]{0:T(256)S(1)} %bitcast.168, f32[256]{0:T(256)S(1)} %bitcast.170, ...), kind=kLoop, calls=%fused_computation.199 | loop fusion | flops 17299456 | bytes 9520128 | tf_op jit(solution)/shard_map/reduce_sum | solution.py:127
  36.8 19.3 %fusion.2 = (bf16[2048,1024]{1,0:T(8,128)(2,1)S(1)}, f32[2048,1024]{1,0:T(8,128)S(1)}) fusion(f32[1024]{0:T(1024)S(1)} %copy-done.19, bf16[2048,256]{1,0:T(8,128)(2,1)S(1)} %bitcast.154, bf16[256,1024]{1,0:T(8,128)(2,1)S(1)} %copy-done), kind=kOutput, calls=%fused_computation.8 | convolution fusion | flops 1212153856 | bytes 14159872 | tf_op jit(solution)/shard_map/dot_general | solution.py:132
  56.2 3.1 %fusion.58 = (f32[256]{0:T(256)}, bf16[2048,256]{1,0:T(8,128)(2,1)}, bf16[2048,256]{1,0:T(8,128)(2,1)S(1)}) fusion(bf16[1,2,32,32,256]{4,3,2,1,0:T(8,128)(2,1)S(1)} %copy-done.6, f32[256]{0:T(256)S(1)} %copy-done.20, bf16[1,2,32,32,256]{4,3,2,1,0:T(8,128)(2,1)S(1)} %copy-done.5, bf16[2048,1024]{1,0:T(8,128)(2,1)S(1)} %get-tuple-element.128, ...), kind=kOutput, calls=%fused_computation.102 | convolution fusion | flops 1078460160 | bytes 8914944 | tf_op jit(solution)/shard_map/dot_general | solution.py:134
  59.3 5.5 %convert_reduce_fusion = (f32[1024]{0:T(1024)}, bf16[2048,1024]{1,0:T(8,128)(2,1)S(1)}) fusion(f32[2048,1024]{1,0:T(8,128)S(1)} %get-tuple-element.129, f32[1024]{0:T(1024)S(1)} %copy-done.19, bf16[2048,256]{1,0:T(8,128)(2,1)S(1)} %get-tuple-element.86, bf16[1024,256]{1,0:T(8,128)(2,1)S(1)} %copy-done.18), kind=kOutput, calls=%fused_computation.15 | convolution fusion | flops 1101003776 | bytes 14163968 | tf_op jit(solution)/shard_map/dot_general | solution.py:146
  64.8 1.4 multiply_reduce_fusion.3
  66.7 1.1 multiply_reduce_fusion
  68.1 8.5 %fusion.48 = (f32[256]{0:T(256)S(1)}, f32[256]{0:T(256)S(1)}, f32[256]{0:T(256)S(1)}, f32[256]{0:T(256)S(1)}, f32[256]{0:T(256)S(1)}, /*index=5*/f32[256]{0:T(25...) fusion(bf16[1,2,33,34,256]{4,3,2,1,0:T(8,128)(2,1)} %copy-done.2, ...), kind=kLoop, calls=%fused_computation.89 | loop fusion | flops 20969216 | bytes 13740032 | tf_op jit(solution)/shard_map/reduce_sum | solution.py:182
  76.6 2.8 %fusion.24 = f32[1,2,34,34,256]{4,3,2,1,0:T(8,128)S(1)} fusion(f32[1,2,32,32,256]{4,3,2,1,0:T(8,128)S(1)} %get-tuple-element.71, f32[256]{0:T(256)S(1)} %bitcast.181, f32[256]{0:T(256)S(1)} %bitcast.183, f32[256]{0:T(256)S(1)} %bitcast.169, f32[256]{0:T(256)S(1)} %bitcast.171, f32[256]{0:T(256)S(1)} %bitcast.173, f32[256]{0:T(256)S(1)} %bitcast.175, ...), kind=kLoop, calls=%fused_computation.48 | loop fusion | flops 10061824 | bytes 4473856 | tf_op jit(solution)/shard_map/add | solution.py:181
  80.9 2.3 fusion.91
  83.2 2.2 fusion.90
  87.0 41.3 %all-reduce.1 = (f32[256,9]{0,1:T(8,128)S(1)}, f32[256]{0:T(256)}, f32[1024]{0:T(1024)S(1)}, f32[256]{0:T(256)}) all-reduce(f32[256,9]{0,1:T(8,128)S(1)} %stack.109, f32[256]{0:T(256)S(1)} %get-tuple-element.57, f32[1024]{0:T(1024)S(1)} %copy-done.14, f32[256]{0:T(256)} %get-tuple-element.82), channel_id=1, replica_groups=mesh['tile'=4,'rep'=8] {'tile','rep'}, use_global_device_ids=true, to_apply=%region_13.14 | all-reduce | flops 3840 | bytes 30720 | tf_op jit(solution)/shard_map/psum | solution.py:231
  129.7 0.8 pad_maximum_fusion.4
  130.5 7.7 %all_gather.11 = bf16[1,8,4,32,256]{4,3,2,0,1:T(8,128)(2,1)S(1)} all-gather(bf16[1,2,4,32,256]{4,3,2,0,1:T(8,128)(2,1)S(1)} %copy.268), channel_id=1, replica_groups=mesh['tile'=4,'rep'=8] {'tile'}, dimensions={1}, use_global_device_ids=true | all-gather | bytes 655360 | tf_op jit(solution)/shard_map/all_gather | solution.py:215
  138.2 1.1 bitcast_convert_fusion
  139.3 2.5 %gather_fusion.2 = f32[8,32,256]{2,1,0:T(8,128)} fusion(f32[8,4,32,256]{3,2,1,0:T(8,128)} %bitcast_convert_fusion, s32[8]{0:T(128)S(1)} %reshape.574), kind=kCustom, calls=%fused_computation.2 | custom fusion | bytes 524352 | tf_op jit(solution)/shard_map/gather | solution.py:54
  141.8 1.6 rev.43
  143.5 1.1 broadcast_select_fusion
  145.9 1.2 broadcast_multiply_fusion.7
  147.9 0.9 collective-permute-start.1
  149.4 0.8 rev.45
  150.2 1.4 collective-permute-done.1
  152.3 4.5 %fusion.56 = f32[1,2,32,32,256]{4,3,2,1,0:T(8,128)} fusion(f32[1,2,34,34,256]{4,3,2,1,0:T(8,128)S(1)} %fusion.24, bf16[1,2,32,32,256]{4,3,2,1,0:T(8,128)(2,1)} %param.11, f32[2,256]{1,0:T(2,128)S(1)} %bitcast.184, f32[2,256]{1,0:T(2,128)S(1)} %bitcast.185, f32[2,256]{1,0:T(2,128)S(1)} %bitcast.186, f32[2,256]{1,0:T(2,128)S(1)} %bitcast.187, ...), kind=kLoop, calls=%fused_computation.98 | loop fusion | flops 9437184 | bytes 5528576 | tf_op jit(solution)/shard_map/add | solution.py:110
  156.9 64.4 %all-reduce.5.cloned.1.call-done = (f32[256,1024]{1,0:T(8,128)}, f32[1024,256]{1,0:T(8,128)}) async-done(((f32[256,1024]{1,0:T(8,128)}, f32[1024,256]{1,0:T(8,128)}), (f32[256,1024]{1,0:T(8,128)}, f32[1024,256]{1,0:T(8,128)})) %all-reduce.5.cloned.1.call-update) | async-done | bytes 2097168 | tf_op jit(solution)/shard_map/psum | solution.py:231
  221.3 2.4 %broadcast_multiply_fusion = f32[1024,256]{1,0:T(8,128)} fusion(f32[1024,256]{1,0:T(8,128)} %get-tuple-element.70), kind=kLoop, calls=%fused_computation.118 | loop fusion | flops 262144 | bytes 2097152 | tf_op jit(solution)/shard_map/mul | solution.py:241
  223.6 1.1 broadcast_multiply_fusion.1
  (125 shorter events, 13.6 us)
Async XLA Ops:
  7.2 29.6 %copy-start = (bf16[256,1024]{1,0:T(8,128)(2,1)S(1)}, bf16[256,1024]{1,0:T(8,128)(2,1)}, u32[]{:S(2)}) copy-start(bf16[256,1024]{1,0:T(8,128)(2,1)} %param.16) | copy-start | bytes 1572868
  7.2 21.2 %copy-start.4 = (bf16[1,2,32,32,256]{4,3,2,1,0:T(8,128)(2,1)S(1)}, bf16[1,2,32,32,256]{4,3,2,1,0:T(8,128)(2,1)}, u32[]{:S(2)}) copy-start(bf16[1,2,32,32,256]{4,3,2,1,0:T(8,128)(2,1)} %param.10) | copy-start | bytes 3145732
  7.2 21.1 %copy-start.13 = (f32[256,9]{0,1:T(8,128)S(1)}, f32[256,9]{0,1:T(8,128)}, u32[]{:S(2)}) copy-start(f32[256,9]{0,1:T(8,128)} %param.14) | copy-start | bytes 27652
  7.2 214.1 %all-reduce.5.cloned.1.call-start = ((), (), s32[]{:S(2)}) async-start(), calls=%async_computation | async-start | bytes 4194304 | tf_op jit(solution)/shard_map/psum | solution.py:231
  11.4 16.5 %copy-start.15 = (pred[2,4]{1,0:T(4,128)(4,1)}, pred[2,4]{1,0:T(4,128)(4,1)S(1)}, u32[]{:S(2)}) copy-start(pred[2,4]{1,0:T(4,128)(4,1)S(1)} %compare_bitcast_fusion) | copy-start | bytes 28
  30.1 5.2 %copy-start.1 = (bf16[1,2,33,34,256]{4,3,2,1,0:T(8,128)(2,1)}, bf16[1,2,33,34,256]{4,3,2,1,0:T(8,128)(2,1)S(1)}, u32[]{:S(2)}) copy-start(bf16[1,2,33,34,256]{4,3,2,1,0:T(8,128)(2,1)S(1)} %get-tuple-element.84) | copy-start | bytes 3446788
  30.1 5.2 %copy-start.2 = (bf16[1,2,33,34,256]{4,3,2,1,0:T(8,128)(2,1)}, bf16[1,2,33,34,256]{4,3,2,1,0:T(8,128)(2,1)S(1)}, u32[]{:S(2)}) copy-start(bf16[1,2,33,34,256]{4,3,2,1,0:T(8,128)(2,1)S(1)} %get-tuple-element.85) | copy-start | bytes 3446788
  30.1 5.9 %copy-start.10 = (f32[256]{0:T(256)S(1)}, f32[256]{0:T(256)}, u32[]{:S(2)}) copy-start(f32[256]{0:T(256)} %param.15) | copy-start | bytes 3076
  35.3 1.4 copy-start.19
  36.7 19.4 %copy-start.8 = (bf16[1,2,32,32,256]{4,3,2,1,0:T(8,128)(2,1)}, bf16[1,2,32,32,256]{4,3,2,1,0:T(8,128)(2,1)S(1)}, u32[]{:S(2)}) copy-start(bf16[1,2,32,32,256]{4,3,2,1,0:T(8,128)(2,1)S(1)} %multiply_convert_fusion) | copy-start | bytes 3145732
  36.8 19.4 %copy-start.5 = (bf16[1,2,32,32,256]{4,3,2,1,0:T(8,128)(2,1)S(1)}, bf16[1,2,32,32,256]{4,3,2,1,0:T(8,128)(2,1)}, u32[]{:S(2)}) copy-start(bf16[1,2,32,32,256]{4,3,2,1,0:T(8,128)(2,1)} %param.10) | copy-start | bytes 3145732
  36.8 19.4 %copy-start.6 = (bf16[1,2,32,32,256]{4,3,2,1,0:T(8,128)(2,1)S(1)}, bf16[1,2,32,32,256]{4,3,2,1,0:T(8,128)(2,1)}, u32[]{:S(2)}) copy-start(bf16[1,2,32,32,256]{4,3,2,1,0:T(8,128)(2,1)} %param.11) | copy-start | bytes 3145732
  36.8 19.4 %copy-start.18 = (bf16[1024,256]{1,0:T(8,128)(2,1)S(1)}, bf16[1024,256]{1,0:T(8,128)(2,1)}, u32[]{:S(2)}) copy-start(bf16[1024,256]{1,0:T(8,128)(2,1)} %param.18) | copy-start | bytes 1572868
  36.8 19.4 %copy-start.20 = (f32[256]{0:T(256)S(1)}, f32[256]{0:T(256)}, u32[]{:S(2)}) copy-start(f32[256]{0:T(256)} %param.19) | copy-start | bytes 3076
  56.2 3.2 %copy-start.23 = (bf16[2048,1024]{1,0:T(8,128)(2,1)}, bf16[2048,1024]{1,0:T(8,128)(2,1)S(1)}, u32[]{:S(2)}) copy-start(bf16[2048,1024]{1,0:T(8,128)(2,1)S(1)} %get-tuple-element.128) | copy-start | bytes 12582916
  59.3 5.5 %copy-start.25 = (bf16[2048,256]{1,0:T(8,128)(2,1)}, bf16[2048,256]{1,0:T(8,128)(2,1)S(1)}, u32[]{:S(2)}) copy-start(bf16[2048,256]{1,0:T(8,128)(2,1)S(1)} %get-tuple-element.86) | copy-start | bytes 3145732
  64.8 1.9 copy-start.21
  66.7 1.3 copy-start.3
  68.1 12.8 %copy-start.26 = (bf16[2048,256]{1,0:T(8,128)(2,1)S(1)}, bf16[2048,256]{1,0:T(8,128)(2,1)}, u32[]{:S(2)}) copy-start(bf16[2048,256]{1,0:T(8,128)(2,1)} %copy-done.25) | copy-start | bytes 3145732
  76.6 4.4 %copy-start.24 = (bf16[2048,1024]{1,0:T(8,128)(2,1)S(1)}, bf16[2048,1024]{1,0:T(8,128)(2,1)}, u32[]{:S(2)}) copy-start(bf16[2048,1024]{1,0:T(8,128)(2,1)} %copy-done.23) | copy-start | bytes 12582916
  80.6 2.6 %copy-start.9 = (bf16[1,2,32,32,256]{4,3,2,1,0:T(8,128)(2,1)S(1)}, bf16[1,2,32,32,256]{4,3,2,1,0:T(8,128)(2,1)}, u32[]{:S(2)}) copy-start(bf16[1,2,32,32,256]{4,3,2,1,0:T(8,128)(2,1)} %copy-done.8) | copy-start | bytes 3145732
  80.6 2.6 %copy-start.22 = (bf16[2048,1024]{1,0:T(8,128)(2,1)S(1)}, bf16[2048,1024]{1,0:T(8,128)(2,1)}, u32[]{:S(2)}) copy-start(bf16[2048,1024]{1,0:T(8,128)(2,1)} %copy-done.21) | copy-start | bytes 12582916
  80.6 66.6 %collective-permute-start = (bf16[1,1,2,4,256]{4,3,2,1,0:T(4,128)(2,1)}, bf16[1,1,2,4,256]{4,3,2,1,0:T(4,128)(2,1)}, u32[]{:S(2)}, u32[]{:S(2)}) collective-permute-start(bf16[1,1,2,4,256]{4,3,2,1,0:T(4,128)(2,1)} %pad_maximum_fusion.8), channel_id=1, source_target_pairs={{0,8},{8,0},{16,24},{24,16},{1,9},{9,1},{17,25},{25,17},{2,10},{10... | collective-permute-start | bytes 12296 | tf_op jit(solution)/shard_map/ppermute | solution.py:22
  85.5 1.5 copy-start.14
  86.1 57.3 %copy-start.16 = (pred[2,4]{1,0:T(4,128)(4,1)S(1)}, pred[2,4]{1,0:T(4,128)(4,1)}, u32[]{:S(2)}) copy-start(pred[2,4]{1,0:T(4,128)(4,1)} %copy-done.15) | copy-start | bytes 28
  86.9 58.4 %copy-start.11 = (pred[32]{0:T(512)(128)(4,1)}, pred[32]{0:T(512)(128)(4,1)S(1)}, u32[]{:S(2)}) copy-start(pred[32]{0:T(512)(128)(4,1)S(1)} %get-tuple-element.138) | copy-start | bytes 100
  86.9 58.4 %copy-start.12 = (pred[32]{0:T(512)(128)(4,1)}, pred[32]{0:T(512)(128)(4,1)S(1)}, u32[]{:S(2)}) copy-start(pred[32]{0:T(512)(128)(4,1)S(1)} %get-tuple-element.139) | copy-start | bytes 100
  129.6 19.2 %copy-start.17 = (f32[256]{0:T(256)S(1)}, f32[256]{0:T(256)}, u32[]{:S(2)}) copy-start(f32[256]{0:T(256)} %get-tuple-element.66) | copy-start | bytes 3076
  147.9 3.7 %collective-permute-start.1 = (bf16[2,1,2,4,256]{4,3,2,0,1:T(4,128)(2,1)S(1)}, bf16[2,1,2,4,256]{4,3,2,0,1:T(4,128)(2,1)S(1)}, u32[]{:S(2)}, u32[]{:S(2)}) collective-permute-start(bf16[2,1,2,4,256]{4,3,2,0,1:T(4,128)(2,1)S(1)} %get-tuple-element.117), channel_id=1, source_target_pairs={{0,16},{8,24},{16,0},{24,8},{1,17},{9,25},{17,1},{25,9},{2,18},{10... | collective-permute-start | bytes 24584 | tf_op jit(solution)/shard_map/ppermute | solution.py:22
  221.3 2.4 %copy-start.7 = (f32[256,1024]{1,0:T(8,128)S(1)}, f32[256,1024]{1,0:T(8,128)}, u32[]{:S(2)}) copy-start(f32[256,1024]{1,0:T(8,128)} %get-tuple-element.69) | copy-start | bytes 3145732
Sparse Core Ops, SparseCore 0:
  85.6 135.6 all-reduce.4
